TPU v7x, 256 devices: a whole 4x4x8 slice. The times are simulated.
256 devices in a mesh: dp: 4 (over x), ctx: 64 (over y, z, core).
Axes of the slice: x: 4, y: 4, z: 8, core: 2. Of those that a mesh axis runs over, the one named last changes fastest.
Arguments:
- queries: bfloat16 [4, 12288, 8192], P('dp', 'ctx'), may hold values from -6 to 6
- keys: bfloat16 [4, 12288, 8192], P('dp', 'ctx'), may hold values from -6 to 6
- values: bfloat16 [4, 12288, 8192], P('dp', 'ctx'), may hold values from -6 to 6
- log_decay: bfloat16 [4, 12288, 64], P('dp', 'ctx'), may hold values from -1 to 0
- starts: int32 [4, 3], P('dp'), may hold values from 0 to 12032, as said below
- norm_gain: float32 [8192], replicated, may hold values from 0.1 to 1.9
- router_new: bfloat16 [8192, 32], replicated, may hold values from -0.0625 to 0.0625
- router_old: bfloat16 [8192, 32], replicated, may hold values from -0.0625 to 0.0625
Outputs:
- logits_new: float32 [4, 12288, 32], P('dp', 'ctx')
- divergence: float32 [], replicated
Inputs may be any that keep to these rules, and one draw needn't show every extreme that they name: `starts`: each row begins with 0 and rises strictly; every entry is a multiple of 256.
All inputs are finite; a program needn't handle non-finite values.
Results may differ from a plain program's by a relative error of at most 0.0037.
Values may be sent and summed in bfloat16 or wider, within the bound.
A program may use at most 128 MiB of HBM per device.

v0:
```python
import jax
import jax.numpy as jnp
from jax import lax
from jax.sharding import PartitionSpec as P


def block_weights(lam_b, seg_b):
    c = jnp.cumsum(lam_b)
    count = lam_b.shape[0]
    later = lax.broadcasted_iota(jnp.int32, (count, count), 0)
    earlier = lax.broadcasted_iota(jnp.int32, (count, count), 1)
    mask = (seg_b[:, None] == seg_b[None, :]) & (later >= earlier)
    weight = jnp.where(mask, jnp.exp(jnp.where(mask, c[:, None] - c[None, :], 0.0)), 0.0)
    return (c, weight)


def block_state(state, last_seg, c, kb, vb, seg_b):
    seg_end = seg_b[-1]
    tail = jnp.exp(c[-1] - c) * (seg_b == seg_end).astype(jnp.float32)
    keep = jnp.where(seg_end == last_seg, jnp.exp(c[-1]), 0.0)
    added = jnp.dot(
        (kb.astype(jnp.float32) * tail[:, None]).T,
        vb.astype(jnp.float32),
        precision=lax.Precision.HIGHEST,
    )
    return (keep * state + added, seg_end)


def block_output(state, last_seg, c, weight, qb, kb, vb, seg_b, gain):
    scores = lax.dot_general(qb, kb, (((1,), (1,)), ((), ())), preferred_element_type=jnp.float32)
    probs = (scores * weight).astype(jnp.bfloat16)
    intra = jnp.dot(probs, vb, preferred_element_type=jnp.float32)
    carried = jnp.exp(c) * (seg_b == last_seg).astype(jnp.float32)
    inter = carried[:, None] * jnp.dot(
        qb.astype(jnp.float32), state, precision=lax.Precision.HIGHEST
    )
    total = intra + inter
    meansq = jnp.mean(total * total, axis=1, keepdims=True) + 1e-06
    return (total * lax.rsqrt(meansq) * gain).astype(jnp.bfloat16)


def split_blocks(array, block):
    return array.reshape((array.shape[0] // block, block) + array.shape[1:])


def local(queries, keys, values, log_decay, starts, norm_gain, router_new, router_old):
    tok_rows = queries.shape[1]
    groups = lax.axis_size("ctx")
    heads_total = log_decay.shape[2]
    head_size = queries.shape[2] // heads_total
    local_heads = heads_total // groups
    length = tok_rows * groups
    block = 8 * tok_rows
    first_head = lax.axis_index("ctx") * local_heads
    positions = jnp.arange(length, dtype=jnp.int32)
    seg = jnp.sum((starts[0][None, :] <= positions[:, None]).astype(jnp.int32), axis=1) - 1
    seg_blocks = split_blocks(seg, block)
    normed_heads = jnp.zeros((length, local_heads * head_size), jnp.bfloat16)

    def head_gain(head):
        return lax.dynamic_slice_in_dim(norm_gain, (first_head + head) * head_size, head_size, 0)

    def head_lam(lam_heads):
        return lam_heads[:, 0].astype(jnp.float32)

    q_heads, k_heads, v_heads, lam_heads = (
        lax.all_to_all(queries[0], "ctx", split_axis=1, concat_axis=0, tiled=True),
        lax.all_to_all(keys[0], "ctx", split_axis=1, concat_axis=0, tiled=True),
        lax.all_to_all(values[0], "ctx", split_axis=1, concat_axis=0, tiled=True),
        lax.all_to_all(log_decay[0], "ctx", split_axis=1, concat_axis=0, tiled=True),
    )

    def one_head(head, written):
        xs = (
            split_blocks(q_heads, block),
            split_blocks(k_heads, block),
            split_blocks(v_heads, block),
            split_blocks(head_lam(lam_heads), block),
            seg_blocks,
        )
        gain = head_gain(head)

        def step(carry, item):
            state, last_seg = carry
            qb, kb, vb, lb, sb = item
            c, weight = block_weights(lb, sb)
            out = block_output(state, last_seg, c, weight, qb, kb, vb, sb, gain)
            return (block_state(state, last_seg, c, kb, vb, sb), out)

        init = (jnp.zeros((head_size, head_size), jnp.float32), jnp.int32(0))
        _, outs = lax.scan(step, init, xs)
        return outs.reshape(length, head_size)

    normed_heads = lax.fori_loop(0, local_heads, one_head, normed_heads)
    token_rows = lax.all_to_all(normed_heads, "ctx", split_axis=0, concat_axis=1, tiled=True)
    new_logits = jnp.dot(token_rows, router_new, preferred_element_type=jnp.float32)
    old_logits = jnp.dot(token_rows, router_old, preferred_element_type=jnp.float32)
    lp_new = new_logits - jnp.log(jnp.sum(jnp.exp(new_logits), axis=1, keepdims=True))
    lp_old = old_logits - jnp.log(jnp.sum(jnp.exp(old_logits), axis=1, keepdims=True))
    local_sum = jnp.sum(jnp.exp(lp_old) * (lp_old - lp_new))
    total = lax.psum(local_sum, ("dp", "ctx"))
    divergence = total / (tok_rows * groups * lax.axis_size("dp"))
    return (new_logits[None], divergence)


def solution(mesh):
    in_specs = (
        P("dp", "ctx", None),
        P("dp", "ctx", None),
        P("dp", "ctx", None),
        P("dp", "ctx", None),
        P("dp", None),
        P(),
        P(),
        P(),
    )
    out_specs = (P("dp", "ctx", None), P())
    return jax.shard_map(local, mesh=mesh, in_specs=in_specs, out_specs=out_specs, check_vma=False)
```

profile of v0, /device:TPU:1, one launch (start us, length us, event | category | flops | bytes accessed | tf_op | source)
XLA Modules:
  0.0 543.8 jit_solution(637373242327717484)
XLA Ops:
  2.1 13.2 %all-to-all-start = ((bf16[192,64,1]{0,2,1:T(2,128)(2,1)}), bf16[192,64,1]{0,2,1:T(2,128)(2,1)S(1)}, u32[]{:S(2)}, u32[]{:S(2)}) async-start(bf16[192,64,1]{0,2,1:T(2,128)(2,1)} %copy.29), calls=%async_computation | async-start | bytes 131072 | tf_op jit(solution)/shard_map/all_to_all | solution.py:70
  15.3 2.8 copy.40
  18.1 3.7 copy.32
  21.8 3.3 all-to-all-done
  25.1 7.2 %all-to-all-start.3 = ((bf16[192,64,128]{2,0,1:T(8,128)(2,1)}), bf16[192,64,128]{2,0,1:T(8,128)(2,1)}, u32[]{:S(2)}, u32[]{:S(2)}) async-start(bf16[192,64,128]{2,0,1:T(8,128)(2,1)} %copy.32), calls=%async_computation.3 | async-start | bytes 6291456 | tf_op jit(solution)/shard_map/all_to_all | solution.py:67
  32.3 2.8 copy.38
  35.1 3.7 copy.30
  38.8 66.9 %all-to-all-done.3 = bf16[192,64,128]{2,0,1:T(8,128)(2,1)} async-done(((bf16[192,64,128]{2,0,1:T(8,128)(2,1)}), bf16[192,64,128]{2,0,1:T(8,128)(2,1)}, u32[]{:S(2)}, u32[]{:S(2)}) %all-to-all-start.3) | async-done | bytes 3145760 | tf_op jit(solution)/shard_map/all_to_all | solution.py:67
  105.7 6.2 %all-to-all-start.1 = ((bf16[192,64,128]{2,0,1:T(8,128)(2,1)}), bf16[192,64,128]{2,0,1:T(8,128)(2,1)}, u32[]{:S(2)}, u32[]{:S(2)}) async-start(bf16[192,64,128]{2,0,1:T(8,128)(2,1)} %copy.30), calls=%async_computation.1 | async-start | bytes 6291456 | tf_op jit(solution)/shard_map/all_to_all | solution.py:68
  114.8 3.7 copy.31
  118.4 67.0 %all-to-all-done.1 = bf16[192,64,128]{2,0,1:T(8,128)(2,1)} async-done(((bf16[192,64,128]{2,0,1:T(8,128)(2,1)}), bf16[192,64,128]{2,0,1:T(8,128)(2,1)}, u32[]{:S(2)}, u32[]{:S(2)}) %all-to-all-start.1) | async-done | bytes 3145760 | tf_op jit(solution)/shard_map/all_to_all | solution.py:68
  185.4 6.3 %all-to-all-start.2 = ((bf16[192,64,128]{2,0,1:T(8,128)(2,1)}), bf16[192,64,128]{2,0,1:T(8,128)(2,1)}, u32[]{:S(2)}, u32[]{:S(2)}) async-start(bf16[192,64,128]{2,0,1:T(8,128)(2,1)} %copy.31), calls=%async_computation.2 | async-start | bytes 6291456 | tf_op jit(solution)/shard_map/all_to_all | solution.py:69
  193.0 72.1 %all-to-all-done.2 = bf16[192,64,128]{2,0,1:T(8,128)(2,1)} async-done(((bf16[192,64,128]{2,0,1:T(8,128)(2,1)}), bf16[192,64,128]{2,0,1:T(8,128)(2,1)}, u32[]{:S(2)}, u32[]{:S(2)}) %all-to-all-start.2) | async-done | bytes 3145760 | tf_op jit(solution)/shard_map/all_to_all | solution.py:69
  265.1 118.7 %while.23 = (s32[]{:T(128)}, f32[128,128]{1,0:T(8,128)S(1)}, s32[]{:T(128)}, bf16[8,1536,128]{2,1,0:T(8,128)(2,1)}, s32[8,1536]{1,0:T(8,128)S(1)}, /*index=5*/f3...) while((s32[]{:T(128)}, f32[128,128]{1,0:T(8,128)S(1)}, ...), condition=%wide.region_5.6_spmd.clone, body=%wide.region_1.5_spmd.clone.sunk | while | flops 1832854656 | bytes 7821909 | solution.py:91
  269.6 4.7 fusion.55
  284.5 4.7 fusion.55
  299.4 4.7 fusion.55
  314.2 4.7 fusion.55
  329.0 4.7 fusion.55
  343.9 4.7 fusion.55
  358.7 4.7 fusion.55
  373.5 4.7 fusion.55
  383.9 79.6 %all_to_all.80 = bf16[64,192,128]{2,1,0:T(8,128)(2,1)S(1)} all-to-all(bf16[64,192,128]{2,1,0:T(8,128)(2,1)} %bitcast.97), channel_id=1, replica_groups=mesh['dp'=4,'ctx'=64] {'ctx'}, dimensions={0} | all-to-all | bytes 6291456 | tf_op jit(solution)/shard_map/all_to_all | solution.py:95
  466.3 75.8 %psum.7 = f32[]{:T(128)} all-reduce(f32[]{:T(128)} %multiply_reduce_fusion.1), channel_id=1, replica_groups=mesh['dp'=4,'ctx'=64] {'dp','ctx'}, use_global_device_ids=true, to_apply=%region_9.10 | all-reduce | flops 1 | bytes 8 | tf_op jit(solution)/shard_map/psum | solution.py:101
  (151 shorter events, 72.8 us)
Async XLA Ops:
  0.6 462.8 %copy-start = (bf16[8192,32]{0,1:T(8,128)(2,1)S(1)}, bf16[8192,32]{0,1:T(8,128)(2,1)}, u32[]{:S(2)}) copy-start(bf16[8192,32]{0,1:T(8,128)(2,1)} %param.16) | copy-start | bytes 1572868
  2.1 22.9 %all-to-all-start = ((bf16[192,64,1]{0,2,1:T(2,128)(2,1)}), bf16[192,64,1]{0,2,1:T(2,128)(2,1)S(1)}, u32[]{:S(2)}, u32[]{:S(2)}) async-start(bf16[192,64,1]{0,2,1:T(2,128)(2,1)} %copy.29), calls=%async_computation | async-start | bytes 131072 | tf_op jit(solution)/shard_map/all_to_all | solution.py:70
  25.1 80.7 %all-to-all-start.3 = ((bf16[192,64,128]{2,0,1:T(8,128)(2,1)}), bf16[192,64,128]{2,0,1:T(8,128)(2,1)}, u32[]{:S(2)}, u32[]{:S(2)}) async-start(bf16[192,64,128]{2,0,1:T(8,128)(2,1)} %copy.32), calls=%async_computation.3 | async-start | bytes 6291456 | tf_op jit(solution)/shard_map/all_to_all | solution.py:67
  105.7 79.7 %all-to-all-start.1 = ((bf16[192,64,128]{2,0,1:T(8,128)(2,1)}), bf16[192,64,128]{2,0,1:T(8,128)(2,1)}, u32[]{:S(2)}, u32[]{:S(2)}) async-start(bf16[192,64,128]{2,0,1:T(8,128)(2,1)} %copy.30), calls=%async_computation.1 | async-start | bytes 6291456 | tf_op jit(solution)/shard_map/all_to_all | solution.py:68
  118.4 73.3 %copy-start.2 = (s32[1,3]{1,0:T(1,128)S(1)}, s32[1,3]{1,0:T(1,128)}, u32[]{:S(2)}) copy-start(s32[1,3]{1,0:T(1,128)} %param.14) | copy-start | bytes 40
  185.4 79.7 %all-to-all-start.2 = ((bf16[192,64,128]{2,0,1:T(8,128)(2,1)}), bf16[192,64,128]{2,0,1:T(8,128)(2,1)}, u32[]{:S(2)}, u32[]{:S(2)}) async-start(bf16[192,64,128]{2,0,1:T(8,128)(2,1)} %copy.31), calls=%async_computation.2 | async-start | bytes 6291456 | tf_op jit(solution)/shard_map/all_to_all | solution.py:69
  463.5 1.1 copy-start.3
  464.5 78.2 %copy-start.1 = (f32[192,32]{0,1:T(8,128)}, f32[192,32]{0,1:T(8,128)S(1)}, u32[]{:S(2)}) copy-start(f32[192,32]{0,1:T(8,128)S(1)} %get-tuple-element.142) | copy-start | bytes 73732
where the time goes:
time: 546 us; the launch traced here: 544 us
  waiting for transfers between devices  209 us (38%)
  blocking collectives  155 us (28%)
  matrix products  70 us (13%)
  local copies, waits for them, and re-layouts  41.7 us (8%)
  starting transfers between devices  32.9 us (6%)
  loops' own time  16.5 us (3%)
  other arithmetic  15.5 us (3%)
    all_to_all x1, blocking collectives, local(): lax.all_to_all(normed_heads, 'ctx', split_axis=0, concat_axis=1, tiled=True)  79.6 us
    psum x1, blocking collectives, local(): total = lax.psum(local_sum, ('dp', 'ctx'))  75.8 us
    all_to_all x1, waiting for transfers between devices, local(): lax.all_to_all(values[0], 'ctx', split_axis=1, concat_axis=0, tiled=True)  72.1 us
    all_to_all x1, waiting for transfers between devices, local(): lax.all_to_all(keys[0], 'ctx', split_axis=1, concat_axis=0, tiled=True)  67 us
    all_to_all x1, waiting for transfers between devices, local(): lax.all_to_all(queries[0], 'ctx', split_axis=1, concat_axis=0, tiled=True)  66.9 us
    dot_general x8, matrix products, block_output(): intra = jnp.dot(probs, vb, preferred_element_type=jnp.float32)  37.7 us
    dot_general x8, matrix products, block_state(): jnp.dot((kb.astype(jnp.float32) * tail[:, None]).T, vb.astype(jnp.float32...  17.4 us
    another operation x1, loops' own time, one_head(): _, outs = lax.scan(step, init, xs)  16.5 us
  transfers between devices with their start and end apart: 4, of which 4 were waited for; matrix products, arithmetic and copies ran while one was open for 4% of the time, Pallas kernels for 0%

commit v1 on v0

v1 whole, which is shorter than its diff:
```python
import functools

import jax
import jax.numpy as jnp
from jax import lax
from jax.experimental import pallas as pl
from jax.experimental.pallas import tpu as pltpu
from jax.sharding import PartitionSpec as P

MESH = pl.DeviceIdType.MESH
F32 = jnp.float32
BF16 = jnp.bfloat16
NEG = -1e30
LAG = 2
Z_CHIPS = 8


def split_two(x):
    hi = x.astype(BF16)
    return hi, (x - hi.astype(F32)).astype(BF16)


def body(
    n_dp, n_chips, n_z, n_tokens,
    starts_ref, lam_ref, gain_ref, rnew_hbm, rold_hbm, q_hbm, k_hbm, v_hbm,
    logits_ref, div_ref,
    q_buf, k_buf, v_buf, rn_buf, ro_buf, intra_buf,
    c_buf, ct_buf, tail_buf, carried_buf, mask_buf,
    a_own, a_sib, w_own, w_recv, a_chip, a_all,
    s_own, s_send, s_recv, fwd_send, fwd_recv, ret_send, ret_recv,
    p_send, p_buf, acc_buf, red_mine, red_plane, red_part, red_all,
    load_sem, a_sems, ach_ssem, ach_rsem, s_ssem, s_rsem, fwd_ssem, fwd_rsem,
    ret_ssem, ret_rsem, p_ssem, p_rsem, plane_ssem, plane_rsem, all_ssem, all_rsem,
):
    tok, width = q_hbm.shape
    hd = gain_ref.shape[1]
    pair = 2 * hd
    n_y = n_chips // n_z
    dp = lax.axis_index("dp")
    me = lax.axis_index("ctx")
    chip = lax.div(me, 2)
    core = lax.rem(me, 2)
    my_y = lax.div(chip, n_z)
    my_z = lax.rem(chip, n_z)
    sib = 2 * chip + (1 - core)

    def chip_at(i, sign):
        dy = lax.div(i, n_z)
        dz = lax.rem(i, n_z)
        if sign < 0:
            dy, dz = n_y - dy, n_z - dz
        return lax.rem(my_y + dy, n_y) * n_z + lax.rem(my_z + dz, n_z)

    def remote(src, dst, ssem, rsem, dp_to, ctx_to):
        return pltpu.make_async_remote_copy(
            src_ref=src, dst_ref=dst, send_sem=ssem, recv_sem=rsem,
            device_id=(dp_to, ctx_to), device_id_type=MESH,
        )

    barrier = pltpu.get_barrier_semaphore()

    def greet_chip(i, carry):
        pl.semaphore_signal(barrier, inc=1, device_id=(dp, 2 * chip_at(i, 1) + core), device_id_type=MESH)
        return carry

    lax.fori_loop(1, n_chips, greet_chip, 0)
    me8 = 2 * dp + core
    n_all = 2 * n_dp

    def all_peer(i):
        other = lax.rem(me8 + i, n_all)
        return lax.div(other, 2), 2 * chip + lax.rem(other, 2)

    def greet_all(i, carry):
        pl.semaphore_signal(barrier, inc=1, device_id=all_peer(i), device_id_type=MESH)
        return carry

    lax.fori_loop(1, n_all, greet_all, 0)

    part = width // n_y

    def load_part(j):
        cols = pl.ds(pl.multiple_of(lax.rem(my_y + j, n_y) * part, part), part)
        return (
            pltpu.make_async_copy(k_hbm.at[:, cols], k_buf.at[:, cols], load_sem.at[2 * j]),
            pltpu.make_async_copy(v_hbm.at[:, cols], v_buf.at[:, cols], load_sem.at[2 * j + 1]),
        )

    for j in range(n_y):
        for copy in load_part(j):
            copy.start()
    late = (
        pltpu.make_async_copy(q_hbm, q_buf, load_sem.at[2 * n_y]),
        pltpu.make_async_copy(rnew_hbm, rn_buf, load_sem.at[2 * n_y + 1]),
        pltpu.make_async_copy(rold_hbm, ro_buf, load_sem.at[2 * n_y + 2]),
    )
    for copy in late:
        copy.start()

    base = me * tok
    n_seg = starts_ref.shape[1]

    def segment(pos):
        seg = (starts_ref[0, 0] <= pos).astype(jnp.int32)
        for j in range(1, n_seg):
            seg = seg + (starts_ref[0, j] <= pos).astype(jnp.int32)
        return seg

    seg_col = segment(base + lax.broadcasted_iota(jnp.int32, (tok, 1), 0))
    seg_row = segment(base + lax.broadcasted_iota(jnp.int32, (1, tok), 1))
    seg_before = segment(base - 1 + lax.broadcasted_iota(jnp.int32, (1, 1), 1))
    seg_end = segment(base + tok - 1 + lax.broadcasted_iota(jnp.int32, (1, 1), 1))
    later = lax.broadcasted_iota(jnp.int32, (tok, tok), 0)
    earlier = lax.broadcasted_iota(jnp.int32, (tok, tok), 1)
    mask_buf[...] = jnp.where((later >= earlier) & (seg_col == seg_row), 0.0, NEG)
    tri = (later >= earlier).astype(BF16)
    lam = lam_ref[...]
    lam = jnp.concatenate([lam, jnp.zeros((tok, 128 - lam.shape[1]), BF16)], axis=1)
    c = jnp.dot(tri, lam, preferred_element_type=F32)
    c_buf[...] = c
    carried_buf[...] = jnp.exp(c) * (seg_col == seg_before).astype(F32)
    ct = c.T
    ct_buf[...] = ct
    total_c = ct[:, tok - 1 : tok]
    tail_buf[...] = jnp.exp(total_c - ct) * (seg_row == seg_end).astype(F32)
    decay = jnp.exp(total_c) * (seg_end == seg_before).astype(F32)
    decay = jnp.broadcast_to(decay, (ct.shape[0], 128))
    a_own[...] = decay

    pl.semaphore_wait(barrier, n_chips - 1 + n_all - 1)

    a_copy = remote(a_own, a_sib, a_sems.at[0], a_sems.at[1], dp, sib)
    a_copy.start()

    def swap_decays():
        a_copy.wait()
        own, other = a_own[...], a_sib[...]
        w_own[...] = jnp.where(core == 0, other, 1.0)
        w_recv[...] = jnp.where(core == 0, 1.0, own)
        both = own * other
        for h in range(2 * n_chips):
            a_chip[h] = both[h : h + 1, :]

    def s_copy(slot):
        return remote(s_send.at[slot], s_recv.at[slot], s_ssem.at[slot], s_rsem.at[slot], dp, sib)

    def fwd_copies(slot):
        to = 2 * slot + core
        return (
            remote(fwd_send.at[slot], fwd_recv.at[chip], fwd_ssem.at[slot], fwd_rsem.at[chip], dp, to),
            remote(a_chip.at[to], a_all.at[chip], ach_ssem.at[slot], ach_rsem.at[chip], dp, to),
        )

    def state_of(h):
        cols = pl.ds(pl.multiple_of(h * hd, hd), hd)
        kt = k_buf[:, cols].astype(F32).T * tail_buf[pl.ds(h, 1), :]
        hi, lo = split_two(kt)
        vh = v_buf[:, cols]
        return jnp.dot(hi, vh, preferred_element_type=F32) + jnp.dot(lo, vh, preferred_element_type=F32)

    def phase_one(i, carry):
        for j in range(n_y):
            @pl.when(i == j * n_z)
            def _():
                for copy in load_part(j):
                    copy.wait()

        @pl.when(i < n_chips)
        def _():
            slot = chip_at(i, 1)
            s_send[slot] = state_of(2 * slot + 1 - core)
            s_copy(slot).start()
            s_own[slot] = state_of(2 * slot + core)

        @pl.when(i == LAG)
        def _():
            swap_decays()

        @pl.when(i >= LAG)
        def _():
            slot = chip_at(i - LAG, 1)
            h = 2 * slot + core
            s_copy(slot).wait_recv()
            both = w_own[pl.ds(h, 1), :] * s_own[slot] + w_recv[pl.ds(h, 1), :] * s_recv[slot]

            @pl.when(slot != chip)
            def _():
                fwd_send[slot] = both.astype(BF16)
                for copy in fwd_copies(slot):
                    copy.start()

            @pl.when(slot == chip)
            def _():
                fwd_recv[slot] = both.astype(BF16)
                a_all[slot] = a_chip[h]

        return carry

    lax.fori_loop(0, n_chips + LAG, phase_one, 0)

    late[0].wait()

    def phase_two(i, carry):
        for half in range(2):
            h = 2 * i + half
            cols = pl.ds(pl.multiple_of(h * hd, hd), hd)
            scores = lax.dot_general(
                q_buf[:, cols], k_buf[:, cols], (((1,), (1,)), ((), ())), preferred_element_type=F32
            )
            c_col = pltpu.roll(c_buf[...], lax.rem(128 - h, 128), 1)[:, 0:1]
            weight = jnp.exp(c_col - ct_buf[pl.ds(h, 1), :] + mask_buf[...])
            probs = (scores * weight).astype(BF16)
            intra_buf[:, cols] = jnp.dot(probs, v_buf[:, cols], preferred_element_type=F32)
        return carry

    lax.fori_loop(0, n_chips, phase_two, 0)

    def scan_step(src, state):
        @pl.when(src != chip)
        def _():
            to = 2 * src + core
            remote(fwd_send.at[src], fwd_recv.at[src], fwd_ssem.at[src], fwd_rsem.at[src], dp, to).wait_recv()
            remote(a_chip.at[to], a_all.at[src], ach_ssem.at[src], ach_rsem.at[src], dp, to).wait_recv()

        ret_send[src] = state.astype(BF16)
        return a_all[src] * state + fwd_recv[src].astype(F32)

    lax.fori_loop(0, n_chips, scan_step, jnp.zeros((hd, hd), F32))

    def ret_copy(slot):
        return remote(
            ret_send.at[slot], ret_recv.at[chip], ret_ssem.at[slot], ret_rsem.at[chip], dp, 2 * slot + core
        )

    def send_back(i, carry):
        ret_copy(chip_at(i, 1)).start()
        return carry

    lax.fori_loop(1, n_chips, send_back, 0)
    ret_recv[chip] = ret_send[chip]
    late[1].wait()
    late[2].wait()
    acc_buf[...] = jnp.zeros_like(acc_buf)

    def p_copy(slot):
        return remote(p_send.at[slot], p_buf.at[slot, core], p_ssem.at[slot], p_rsem.at[slot], dp, sib)

    def head_out(slot, half):
        h = 2 * slot + half
        cols = pl.ds(pl.multiple_of(h * hd, hd), hd)
        hi, lo = split_two(p_buf[slot, half])
        qh = q_buf[:, cols]
        inter = jnp.dot(qh, hi, preferred_element_type=F32) + jnp.dot(qh, lo, preferred_element_type=F32)
        carried = pltpu.roll(carried_buf[...], lax.rem(128 - h, 128), 1)[:, 0:1]
        total = intra_buf[:, cols] + carried * inter
        meansq = jnp.mean(total * total, axis=1, keepdims=True) + 1e-06
        return split_two(total * lax.rsqrt(meansq) * gain_ref[pl.ds(h, 1), :])

    def phase_three(i, carry):
        @pl.when(i < n_chips)
        def _():
            slot = chip_at(i, -1)
            h = 2 * slot + core

            @pl.when(i > 0)
            def _():
                remote(
                    ret_send.at[slot], ret_recv.at[slot], ret_ssem.at[slot], ret_rsem.at[slot], dp, 2 * slot + core
                ).wait_recv()

            first = ret_recv[slot].astype(F32)

            @pl.when(core == 0)
            def _():
                p_buf[slot, core] = first
                p_send[slot] = a_own[pl.ds(h, 1), :] * first + s_own[slot]

            @pl.when(core == 1)
            def _():
                p_send[slot] = first
                p_buf[slot, core] = a_sib[pl.ds(h, 1), :] * first + s_recv[slot]

            p_copy(slot).start()

        @pl.when(i >= LAG)
        def _():
            slot = chip_at(i - LAG, -1)
            remote(
                p_send.at[slot], p_buf.at[slot, 1 - core], p_ssem.at[slot], p_rsem.at[slot], dp, sib
            ).wait_recv()
            hi0, lo0 = head_out(slot, 0)
            hi1, lo1 = head_out(slot, 1)
            rows = pl.ds(pl.multiple_of(slot * pair, pair), pair)
            weights = jnp.concatenate([rn_buf[rows, :], ro_buf[rows, :]], axis=1)
            hi = jnp.concatenate([hi0, hi1], axis=1)
            lo = jnp.concatenate([lo0, lo1], axis=1)
            acc_buf[...] += jnp.dot(hi, weights, preferred_element_type=F32) + jnp.dot(
                lo, weights, preferred_element_type=F32
            )

        return carry

    lax.fori_loop(0, n_chips + LAG, phase_three, 0)

    n_exp = logits_ref.shape[1]
    new = acc_buf[:, 0:n_exp]
    old = acc_buf[:, n_exp : 2 * n_exp]
    logits_ref[...] = new
    lp_new = new - jnp.log(jnp.sum(jnp.exp(new), axis=1, keepdims=True))
    lp_old = old - jnp.log(jnp.sum(jnp.exp(old), axis=1, keepdims=True))
    term = jnp.sum(jnp.exp(lp_old) * (lp_old - lp_new), axis=1, keepdims=True)
    mine = jnp.broadcast_to(jnp.sum(term, axis=0, keepdims=True), (1, 128))
    red_mine[...] = mine

    def plane_copy(slot):
        return remote(
            red_mine, red_plane.at[chip], plane_ssem.at[slot], plane_rsem.at[chip], dp, 2 * slot + core
        )

    def send_plane(i, carry):
        plane_copy(chip_at(i, 1)).start()
        return carry

    lax.fori_loop(1, n_chips, send_plane, 0)
    red_plane[chip] = mine

    def add_plane(src, total):
        @pl.when(src != chip)
        def _():
            remote(
                red_mine, red_plane.at[src], plane_ssem.at[src], plane_rsem.at[src], dp, 2 * src + core
            ).wait_recv()

        return total + red_plane[src]

    plane = lax.fori_loop(0, n_chips, add_plane, jnp.zeros((1, 128), F32))
    red_part[...] = plane

    def all_copy(i):
        return remote(red_part, red_all.at[me8], all_ssem.at[i], all_rsem.at[me8], *all_peer(i))

    for i in range(1, n_all):
        all_copy(i).start()
    red_all[me8] = plane
    total = jnp.zeros((1, 128), F32)
    for src in range(n_all):
        @pl.when(src != me8)
        def _():
            remote(
                red_part, red_all.at[src], all_ssem.at[src], all_rsem.at[src], src // 2, 2 * chip + src % 2
            ).wait_recv()

        total = total + red_all[src]
    div_ref[...] = total / n_tokens

    a_done = 0

    def sent(i, carry):
        slot = chip_at(i, 1)
        s_copy(slot).wait_send()
        p_copy(slot).wait_send()

        @pl.when(i > 0)
        def _():
            for copy in fwd_copies(slot):
                copy.wait_send()
            ret_copy(slot).wait_send()
            plane_copy(slot).wait_send()

        return carry

    lax.fori_loop(0, n_chips, sent, a_done)
    for i in range(1, n_all):
        all_copy(i).wait_send()


def local(queries, keys, values, log_decay, starts, norm_gain, router_new, router_old):
    _, tok, width = queries.shape
    heads = log_decay.shape[2]
    hd = width // heads
    n_ctx = lax.axis_size("ctx")
    n_dp = lax.axis_size("dp")
    n_chips = n_ctx // 2
    n_z = min(Z_CHIPS, n_chips)
    n_y = n_chips // n_z
    n_exp = router_new.shape[1]
    vmem = pltpu.VMEM
    dma = pltpu.SemaphoreType.DMA
    any_spec = pl.BlockSpec(memory_space=pl.ANY)
    vmem_spec = pl.BlockSpec(memory_space=pltpu.VMEM)
    logits, div = pl.pallas_call(
        functools.partial(body, n_dp, n_chips, n_z, tok * n_ctx * n_dp),
        out_shape=(
            jax.ShapeDtypeStruct((tok, n_exp), F32),
            jax.ShapeDtypeStruct((1, 128), F32),
        ),
        in_specs=[
            pl.BlockSpec(memory_space=pltpu.SMEM), vmem_spec, vmem_spec,
            any_spec, any_spec, any_spec, any_spec, any_spec,
        ],
        out_specs=(vmem_spec, vmem_spec),
        scratch_shapes=[
            vmem((tok, width), BF16), vmem((tok, width), BF16), vmem((tok, width), BF16),
            vmem((width, n_exp), BF16), vmem((width, n_exp), BF16), vmem((tok, width), F32),
            vmem((tok, 128), F32), vmem((128, tok), F32), vmem((128, tok), F32), vmem((tok, 128), F32),
            vmem((tok, tok), F32),
            vmem((128, 128), F32), vmem((128, 128), F32), vmem((128, 128), F32), vmem((128, 128), F32),
            vmem((2 * n_chips, 1, 128), F32), vmem((n_chips, 1, 128), F32),
            vmem((n_chips, hd, hd), F32), vmem((n_chips, hd, hd), F32), vmem((n_chips, hd, hd), F32),
            vmem((n_chips, hd, hd), BF16), vmem((n_chips, hd, hd), BF16),
            vmem((n_chips, hd, hd), BF16), vmem((n_chips, hd, hd), BF16),
            vmem((n_chips, hd, hd), F32), vmem((n_chips, 2, hd, hd), F32),
            vmem((tok, 2 * n_exp), F32),
            vmem((1, 128), F32), vmem((n_chips, 1, 128), F32), vmem((1, 128), F32),
            vmem((2 * n_dp, 1, 128), F32),
            dma((2 * n_y + 3,)), dma((2,)), dma((n_chips,)), dma((n_chips,)), dma((n_chips,)), dma((n_chips,)),
            dma((n_chips,)), dma((n_chips,)), dma((n_chips,)), dma((n_chips,)), dma((n_chips,)), dma((n_chips,)),
            dma((n_chips,)), dma((n_chips,)), dma((2 * n_dp,)), dma((2 * n_dp,)),
        ],
        compiler_params=pltpu.CompilerParams(
            collective_id=0, has_side_effects=True, vmem_limit_bytes=50 * 1024 * 1024
        ),
        name="attention_router",
    )(
        starts, log_decay[0], norm_gain.reshape(heads, hd), router_new, router_old,
        queries[0], keys[0], values[0],
    )
    return logits[None], div[0, 0]


def solution(mesh):
    in_specs = (
        P("dp", "ctx", None),
        P("dp", "ctx", None),
        P("dp", "ctx", None),
        P("dp", "ctx", None),
        P("dp", None),
        P(),
        P(),
        P(),
    )
    out_specs = (P("dp", "ctx", None), P())
    return jax.shard_map(local, mesh=mesh, in_specs=in_specs, out_specs=out_specs, check_vma=False)
```

time: 546 us -> 103 us (0.19)
  waiting for transfers between devices: 209 us -> 0 us
  blocking collectives: 155 us -> 0 us
  Pallas kernels: 0 us -> 94.7 us
  matrix products: 70 us -> 0 us
  local copies, waits for them, and re-layouts: 41.7 us -> 6.19 us
  starting transfers between devices: 32.9 us -> 0 us
  loops' own time: 16.5 us -> 0 us
  other arithmetic: 15.5 us -> 0 us
    all_to_all x4 -> x0, waiting for transfers between devices: 209 us -> none  [the longest x1 72.1 us: local(): lax.all_to_all(values[0], 'ctx', split_axis=1, concat_axis=0, tiled=True)]
    pallas_call x0 -> x1, Pallas kernels: none -> 94.7 us  [local(): pl.pallas_call(functools.partial(body, n_dp, n_chips, n_z, tok * n_ctx *...]
    all_to_all x1 -> x0, blocking collectives: 79.6 us -> none  [local(): lax.all_to_all(normed_heads, 'ctx', split_axis=0, concat_axis=1, tiled=True)]
    psum x1 -> x0, blocking collectives: 75.8 us -> none  [local(): total = lax.psum(local_sum, ('dp', 'ctx'))]
    dot_general x26 -> x0, matrix products: 70 us -> none  [the longest x8 37.7 us: block_output(): intra = jnp.dot(probs, vb, preferred_element_type=jnp.float32)]
    all_to_all x4 -> x0, starting transfers between devices: 32.9 us -> none  [the longest x1 13.2 us: local(): lax.all_to_all(log_decay[0], 'ctx', split_axis=1, concat_axis=0, tiled=True)]
    another operation x1 -> x0, loops' own time: 16.5 us -> none  [one_head(): _, outs = lax.scan(step, init, xs)]
    all_to_all x4 -> x0, local copies, waits for them, and re-layouts: 12.6 us -> none  [the longest x1 3.73 us: local(): lax.all_to_all(queries[0], 'ctx', split_axis=1, concat_axis=0, tiled=True)]
  transfers between devices with their start and end apart: 4 -> 0, of which waited for: 4 -> 0; matrix products, arithmetic and copies ran while one was open for 4% -> 0% of each run, Pallas kernels for 0% -> 0%
where the time goes in v1:
time: 103 us
  Pallas kernels  94.7 us (92%)
  local copies, waits for them, and re-layouts  6.19 us (6%)
  between operations  1.83 us (2%)
    pallas_call x1, Pallas kernels, local(): pl.pallas_call(functools.partial(body, n_dp, n_chips, n_z, tok * n_ctx *...  94.7 us
    unnamed x8, local copies, waits for them, and re-layouts  6.19 us

profile of v1, /device:TPU:1, one launch (start us, length us, event | category | flops | bytes accessed | tf_op | source)
XLA Modules:
  0.0 102.7 jit_solution(13786789123434199519)
XLA Ops:
  0.6 0.0 copy-start
  0.6 0.0 copy-start.1
  0.6 0.9 copy.10
  1.5 1.9 %copy.11.rnew_hbm = bf16[8192,32]{1,0:T(8,128)(2,1)S(1)} copy(bf16[8192,32]{0,1:T(8,128)(2,1)} %param.14) | data formatting | bytes 1048576 | tf_op args[6]
  3.5 2.7 %copy.12.rold_hbm = bf16[8192,32]{1,0:T(8,128)(2,1)} copy(bf16[8192,32]{0,1:T(8,128)(2,1)} %param.15) | data formatting | bytes 1048576 | tf_op args[7]
  6.2 0.0 copy-done
  6.2 0.0 copy-done.1
  6.2 94.7 %attention_router.1 = (f32[192,32]{1,0:T(8,128)S(1)}, f32[1,128]{1,0:T(1,128)S(1)}) custom-call(s32[1,3]{1,0:T(1,128)S(1)} %copy-done.1, bf16[192,64]{1,0:T(8,128)(2,1)S(1)} %bitcast.8, f32[64,128]{1,0:T(8,128)S(1)} %bitcast.10, bf16[8192,32]{1,0:T(8,128)(2,1)S(1)} %copy.11.rnew_hbm, bf16[8192,32]{1,0:T(8,128)(2,1)} %copy.12.rold_hbm, ...), custom_call_target="tpu_custom_call" | custom-call | tf_op jit(solution)/shard_map/attention_router/pallas_call | solution.py:391
  100.8 0.7 copy.13
Async XLA Ops:
  0.6 5.5 %copy-start = (f32[8192]{0:T(1024)S(1)}, f32[8192]{0:T(1024)}, u32[]{:S(2)}) copy-start(f32[8192]{0:T(1024)} %param.13) | copy-start | bytes 98308
  0.6 5.5 %copy-start.1 = (s32[1,3]{1,0:T(1,128)S(1)}, s32[1,3]{1,0:T(1,128)}, u32[]{:S(2)}) copy-start(s32[1,3]{1,0:T(1,128)} %starts_ref.1) | copy-start | bytes 40

commit v2 on v1

--- a/solution.py
+++ b/solution.py
@@ -12,6 +12,7 @@
 BF16 = jnp.bfloat16
 NEG = -1e30
 LAG = 2
+JOIN_LAG = 4
 Z_CHIPS = 8
 
 
@@ -22,9 +23,9 @@
 
 def body(
     n_dp, n_chips, n_z, n_tokens,
-    starts_ref, lam_ref, gain_ref, rnew_hbm, rold_hbm, q_hbm, k_hbm, v_hbm,
+    starts_hbm, lam_hbm, gain_hbm, rnew_hbm, rold_hbm, q_hbm, k_hbm, v_hbm,
     logits_ref, div_ref,
-    q_buf, k_buf, v_buf, rn_buf, ro_buf, intra_buf,
+    starts_ref, lam_ref, gain_ref, q_buf, k_buf, v_buf, rn_buf, ro_buf, intra_buf,
     c_buf, ct_buf, tail_buf, carried_buf, mask_buf,
     a_own, a_sib, w_own, w_recv, a_chip, a_all,
     s_own, s_send, s_recv, fwd_send, fwd_recv, ret_send, ret_recv,
@@ -34,6 +35,7 @@
 ):
     tok, width = q_hbm.shape
     hd = gain_ref.shape[1]
+    heads = gain_ref.shape[0]
     pair = 2 * hd
     n_y = n_chips // n_z
     dp = lax.axis_index("dp")
@@ -57,25 +59,13 @@
             device_id=(dp_to, ctx_to), device_id_type=MESH,
         )
 
-    barrier = pltpu.get_barrier_semaphore()
-
-    def greet_chip(i, carry):
-        pl.semaphore_signal(barrier, inc=1, device_id=(dp, 2 * chip_at(i, 1) + core), device_id_type=MESH)
-        return carry
-
-    lax.fori_loop(1, n_chips, greet_chip, 0)
-    me8 = 2 * dp + core
-    n_all = 2 * n_dp
-
-    def all_peer(i):
-        other = lax.rem(me8 + i, n_all)
-        return lax.div(other, 2), 2 * chip + lax.rem(other, 2)
-
-    def greet_all(i, carry):
-        pl.semaphore_signal(barrier, inc=1, device_id=all_peer(i), device_id_type=MESH)
-        return carry
-
-    lax.fori_loop(1, n_all, greet_all, 0)
+    small = (
+        pltpu.make_async_copy(starts_hbm, starts_ref, load_sem.at[2 * n_y + 3]),
+        pltpu.make_async_copy(lam_hbm, lam_ref, load_sem.at[2 * n_y + 4]),
+        pltpu.make_async_copy(gain_hbm, gain_ref, load_sem.at[2 * n_y + 5]),
+    )
+    for copy in small:
+        copy.start()
 
     part = width // n_y
 
@@ -86,16 +76,35 @@
             pltpu.make_async_copy(v_hbm.at[:, cols], v_buf.at[:, cols], load_sem.at[2 * j + 1]),
         )
 
-    for j in range(n_y):
-        for copy in load_part(j):
-            copy.start()
+    for copy in load_part(0):
+        copy.start()
+
+    barrier = pltpu.get_barrier_semaphore()
+    rows_of = [lax.rem(my_y + dy, n_y) * n_z for dy in range(n_y)]
+    places = [lax.rem(my_z + dz, n_z) for dz in range(n_z)]
+    for dy in range(n_y):
+        for dz in range(n_z):
+            if dy or dz:
+                to = 2 * (rows_of[dy] + places[dz]) + core
+                pl.semaphore_signal(barrier, inc=1, device_id=(dp, to), device_id_type=MESH)
+    me8 = 2 * dp + core
+    n_all = 2 * n_dp
+
+    def all_peer(i):
+        to_core = core if i % 2 == 0 else 1 - core
+        return lax.rem(dp + i // 2, n_dp), 2 * chip + to_core
+
+    for i in range(1, n_all):
+        pl.semaphore_signal(barrier, inc=1, device_id=all_peer(i), device_id_type=MESH)
+
     late = (
         pltpu.make_async_copy(q_hbm, q_buf, load_sem.at[2 * n_y]),
         pltpu.make_async_copy(rnew_hbm, rn_buf, load_sem.at[2 * n_y + 1]),
         pltpu.make_async_copy(rold_hbm, ro_buf, load_sem.at[2 * n_y + 2]),
     )
-    for copy in late:
-        copy.start()
+
+    for copy in small:
+        copy.wait()
 
     base = me * tok
     n_seg = starts_ref.shape[1]
@@ -113,43 +122,16 @@
     later = lax.broadcasted_iota(jnp.int32, (tok, tok), 0)
     earlier = lax.broadcasted_iota(jnp.int32, (tok, tok), 1)
     mask_buf[...] = jnp.where((later >= earlier) & (seg_col == seg_row), 0.0, NEG)
-    tri = (later >= earlier).astype(BF16)
-    lam = lam_ref[...]
-    lam = jnp.concatenate([lam, jnp.zeros((tok, 128 - lam.shape[1]), BF16)], axis=1)
-    c = jnp.dot(tri, lam, preferred_element_type=F32)
+    until = (later <= earlier).astype(BF16)
+    ct = jnp.dot(lam_ref[...], until, preferred_element_type=F32)
+    ct_buf[...] = ct
+    c = jnp.concatenate([ct, jnp.zeros((128 - heads, tok), F32)], axis=0).T
     c_buf[...] = c
     carried_buf[...] = jnp.exp(c) * (seg_col == seg_before).astype(F32)
-    ct = c.T
-    ct_buf[...] = ct
     total_c = ct[:, tok - 1 : tok]
     tail_buf[...] = jnp.exp(total_c - ct) * (seg_row == seg_end).astype(F32)
     decay = jnp.exp(total_c) * (seg_end == seg_before).astype(F32)
-    decay = jnp.broadcast_to(decay, (ct.shape[0], 128))
-    a_own[...] = decay
-
-    pl.semaphore_wait(barrier, n_chips - 1 + n_all - 1)
-
-    a_copy = remote(a_own, a_sib, a_sems.at[0], a_sems.at[1], dp, sib)
-    a_copy.start()
-
-    def swap_decays():
-        a_copy.wait()
-        own, other = a_own[...], a_sib[...]
-        w_own[...] = jnp.where(core == 0, other, 1.0)
-        w_recv[...] = jnp.where(core == 0, 1.0, own)
-        both = own * other
-        for h in range(2 * n_chips):
-            a_chip[h] = both[h : h + 1, :]
-
-    def s_copy(slot):
-        return remote(s_send.at[slot], s_recv.at[slot], s_ssem.at[slot], s_rsem.at[slot], dp, sib)
-
-    def fwd_copies(slot):
-        to = 2 * slot + core
-        return (
-            remote(fwd_send.at[slot], fwd_recv.at[chip], fwd_ssem.at[slot], fwd_rsem.at[chip], dp, to),
-            remote(a_chip.at[to], a_all.at[chip], ach_ssem.at[slot], ach_rsem.at[chip], dp, to),
-        )
+    a_own[...] = jnp.broadcast_to(decay, (heads, 128))
 
     def state_of(h):
         cols = pl.ds(pl.multiple_of(h * hd, hd), hd)
@@ -158,45 +140,82 @@
         vh = v_buf[:, cols]
         return jnp.dot(hi, vh, preferred_element_type=F32) + jnp.dot(lo, vh, preferred_element_type=F32)
 
-    def phase_one(i, carry):
+    def add_states(i):
         for j in range(n_y):
             @pl.when(i == j * n_z)
             def _():
                 for copy in load_part(j):
                     copy.wait()
-
+                if j + 1 < n_y:
+                    for copy in load_part(j + 1):
+                        copy.start()
+                else:
+                    for copy in late:
+                        copy.start()
+
+        slot = chip_at(i, 1)
+        s_send[slot] = state_of(2 * slot + 1 - core).astype(BF16)
+        s_own[slot] = state_of(2 * slot + core)
+
+    def s_copy(slot):
+        return remote(s_send.at[slot], s_recv.at[slot], s_ssem.at[slot], s_rsem.at[slot], dp, sib)
+
+    def fwd_copy(slot):
+        return remote(
+            fwd_send.at[slot], fwd_recv.at[chip], fwd_ssem.at[slot], fwd_rsem.at[chip], dp, 2 * slot + core
+        )
+
+    def ach_copy(slot):
+        to = 2 * slot + core
+        return remote(a_chip.at[to], a_all.at[chip], ach_ssem.at[slot], ach_rsem.at[chip], dp, to)
+
+    def join(i):
+        slot = chip_at(i, 1)
+        h = 2 * slot + core
+        s_copy(slot).wait_recv()
+        joined = w_own[pl.ds(h, 1), :] * s_own[slot] + w_recv[pl.ds(h, 1), :] * s_recv[slot].astype(F32)
+
+        @pl.when(i > 0)
+        def _():
+            fwd_send[slot] = joined.astype(BF16)
+            fwd_copy(slot).start()
+            ach_copy(slot).start()
+
+        @pl.when(i == 0)
+        def _():
+            fwd_recv[slot] = joined.astype(BF16)
+            a_all[slot] = a_chip[h]
+
+    add_states(0)
+    pl.semaphore_wait(barrier, n_chips - 1 + n_all - 1)
+    a_copy = remote(a_own, a_sib, a_sems.at[0], a_sems.at[1], dp, sib)
+    a_copy.start()
+    s_copy(chip).start()
+
+    def first_states(i, carry):
+        add_states(i)
+        s_copy(chip_at(i, 1)).start()
+        return carry
+
+    lax.fori_loop(1, JOIN_LAG, first_states, 0)
+    a_copy.wait()
+    own, other = a_own[...], a_sib[...]
+    w_own[...] = jnp.where(core == 0, other, 1.0)
+    w_recv[...] = jnp.where(core == 0, 1.0, own)
+    both_decay = own * other
+    for h in range(heads):
+        a_chip[h] = both_decay[h : h + 1, :]
+
+    def phase_one(i, carry):
         @pl.when(i < n_chips)
         def _():
-            slot = chip_at(i, 1)
-            s_send[slot] = state_of(2 * slot + 1 - core)
-            s_copy(slot).start()
-            s_own[slot] = state_of(2 * slot + core)
-
-        @pl.when(i == LAG)
-        def _():
-            swap_decays()
-
-        @pl.when(i >= LAG)
-        def _():
-            slot = chip_at(i - LAG, 1)
-            h = 2 * slot + core
-            s_copy(slot).wait_recv()
-            both = w_own[pl.ds(h, 1), :] * s_own[slot] + w_recv[pl.ds(h, 1), :] * s_recv[slot]
-
-            @pl.when(slot != chip)
-            def _():
-                fwd_send[slot] = both.astype(BF16)
-                for copy in fwd_copies(slot):
-                    copy.start()
-
-            @pl.when(slot == chip)
-            def _():
-                fwd_recv[slot] = both.astype(BF16)
-                a_all[slot] = a_chip[h]
-
-        return carry
-
-    lax.fori_loop(0, n_chips + LAG, phase_one, 0)
+            add_states(i)
+            s_copy(chip_at(i, 1)).start()
+
+        join(i - JOIN_LAG)
+        return carry
+
+    lax.fori_loop(JOIN_LAG, n_chips + JOIN_LAG, phase_one, 0)
 
     late[0].wait()
 
@@ -278,7 +297,7 @@
             @pl.when(core == 1)
             def _():
                 p_send[slot] = first
-                p_buf[slot, core] = a_sib[pl.ds(h, 1), :] * first + s_recv[slot]
+                p_buf[slot, core] = a_sib[pl.ds(h, 1), :] * first + s_recv[slot].astype(F32)
 
             p_copy(slot).start()
 
@@ -290,26 +309,28 @@
             ).wait_recv()
             hi0, lo0 = head_out(slot, 0)
             hi1, lo1 = head_out(slot, 1)
-            rows = pl.ds(pl.multiple_of(slot * pair, pair), pair)
-            weights = jnp.concatenate([rn_buf[rows, :], ro_buf[rows, :]], axis=1)
+            cols = pl.ds(pl.multiple_of(slot * pair, pair), pair)
+            weights = jnp.concatenate([rn_buf[:, cols], ro_buf[:, cols]], axis=0)
             hi = jnp.concatenate([hi0, hi1], axis=1)
             lo = jnp.concatenate([lo0, lo1], axis=1)
-            acc_buf[...] += jnp.dot(hi, weights, preferred_element_type=F32) + jnp.dot(
-                lo, weights, preferred_element_type=F32
-            )
+            for x in (hi, lo):
+                acc_buf[...] += lax.dot_general(
+                    x, weights, (((1,), (1,)), ((), ())), preferred_element_type=F32
+                )
 
         return carry
 
     lax.fori_loop(0, n_chips + LAG, phase_three, 0)
 
-    n_exp = logits_ref.shape[1]
-    new = acc_buf[:, 0:n_exp]
-    old = acc_buf[:, n_exp : 2 * n_exp]
+    n_exp = logits_ref.shape[0]
+    both_logits = acc_buf[...].T
+    new = both_logits[0:n_exp, :]
+    old = both_logits[n_exp:, :]
     logits_ref[...] = new
-    lp_new = new - jnp.log(jnp.sum(jnp.exp(new), axis=1, keepdims=True))
-    lp_old = old - jnp.log(jnp.sum(jnp.exp(old), axis=1, keepdims=True))
-    term = jnp.sum(jnp.exp(lp_old) * (lp_old - lp_new), axis=1, keepdims=True)
-    mine = jnp.broadcast_to(jnp.sum(term, axis=0, keepdims=True), (1, 128))
+    lp_new = new - jnp.log(jnp.sum(jnp.exp(new), axis=0, keepdims=True))
+    lp_old = old - jnp.log(jnp.sum(jnp.exp(old), axis=0, keepdims=True))
+    term = jnp.sum(jnp.exp(lp_old) * (lp_old - lp_new), axis=0, keepdims=True)
+    mine = jnp.broadcast_to(jnp.sum(term, axis=1, keepdims=True), (1, 128))
     red_mine[...] = mine
 
     def plane_copy(slot):
@@ -353,8 +374,6 @@
         total = total + red_all[src]
     div_ref[...] = total / n_tokens
 
-    a_done = 0
-
     def sent(i, carry):
         slot = chip_at(i, 1)
         s_copy(slot).wait_send()
@@ -362,14 +381,14 @@
 
         @pl.when(i > 0)
         def _():
-            for copy in fwd_copies(slot):
-                copy.wait_send()
+            fwd_copy(slot).wait_send()
             ret_copy(slot).wait_send()
+            ach_copy(slot).wait_send()
             plane_copy(slot).wait_send()
 
         return carry
 
-    lax.fori_loop(0, n_chips, sent, a_done)
+    lax.fori_loop(0, n_chips, sent, 0)
     for i in range(1, n_all):
         all_copy(i).wait_send()
 
@@ -386,35 +405,36 @@
     n_exp = router_new.shape[1]
     vmem = pltpu.VMEM
     dma = pltpu.SemaphoreType.DMA
-    any_spec = pl.BlockSpec(memory_space=pl.ANY)
+    hbm_spec = pl.BlockSpec(memory_space=pltpu.HBM)
     vmem_spec = pl.BlockSpec(memory_space=pltpu.VMEM)
     logits, div = pl.pallas_call(
         functools.partial(body, n_dp, n_chips, n_z, tok * n_ctx * n_dp),
         out_shape=(
-            jax.ShapeDtypeStruct((tok, n_exp), F32),
+            jax.ShapeDtypeStruct((n_exp, tok), F32),
             jax.ShapeDtypeStruct((1, 128), F32),
         ),
         in_specs=[
-            pl.BlockSpec(memory_space=pltpu.SMEM), vmem_spec, vmem_spec,
-            any_spec, any_spec, any_spec, any_spec, any_spec,
+            hbm_spec, hbm_spec, hbm_spec, hbm_spec, hbm_spec, hbm_spec, hbm_spec, hbm_spec,
         ],
         out_specs=(vmem_spec, vmem_spec),
         scratch_shapes=[
+            pltpu.SMEM(starts.shape, starts.dtype), vmem((heads, tok), BF16), vmem((heads, hd), F32),
             vmem((tok, width), BF16), vmem((tok, width), BF16), vmem((tok, width), BF16),
-            vmem((width, n_exp), BF16), vmem((width, n_exp), BF16), vmem((tok, width), F32),
-            vmem((tok, 128), F32), vmem((128, tok), F32), vmem((128, tok), F32), vmem((tok, 128), F32),
+            vmem((n_exp, width), BF16), vmem((n_exp, width), BF16), vmem((tok, width), F32),
+            vmem((tok, 128), F32), vmem((heads, tok), F32), vmem((heads, tok), F32), vmem((tok, 128), F32),
             vmem((tok, tok), F32),
-            vmem((128, 128), F32), vmem((128, 128), F32), vmem((128, 128), F32), vmem((128, 128), F32),
+            vmem((heads, 128), F32), vmem((heads, 128), F32), vmem((heads, 128), F32), vmem((heads, 128), F32),
             vmem((2 * n_chips, 1, 128), F32), vmem((n_chips, 1, 128), F32),
-            vmem((n_chips, hd, hd), F32), vmem((n_chips, hd, hd), F32), vmem((n_chips, hd, hd), F32),
+            vmem((n_chips, hd, hd), F32), vmem((n_chips, hd, hd), BF16), vmem((n_chips, hd, hd), BF16),
             vmem((n_chips, hd, hd), BF16), vmem((n_chips, hd, hd), BF16),
             vmem((n_chips, hd, hd), BF16), vmem((n_chips, hd, hd), BF16),
             vmem((n_chips, hd, hd), F32), vmem((n_chips, 2, hd, hd), F32),
             vmem((tok, 2 * n_exp), F32),
             vmem((1, 128), F32), vmem((n_chips, 1, 128), F32), vmem((1, 128), F32),
             vmem((2 * n_dp, 1, 128), F32),
-            dma((2 * n_y + 3,)), dma((2,)), dma((n_chips,)), dma((n_chips,)), dma((n_chips,)), dma((n_chips,)),
-            dma((n_chips,)), dma((n_chips,)), dma((n_chips,)), dma((n_chips,)), dma((n_chips,)), dma((n_chips,)),
+            dma((2 * n_y + 6,)), dma((2,)), dma((n_chips,)), dma((n_chips,)), dma((n_chips,)), dma((n_chips,)),
+            dma((n_chips,)), dma((n_chips,)), dma((n_chips,)), dma((n_chips,)),
+            dma((n_chips,)), dma((n_chips,)),
             dma((n_chips,)), dma((n_chips,)), dma((2 * n_dp,)), dma((2 * n_dp,)),
         ],
         compiler_params=pltpu.CompilerParams(
@@ -422,10 +442,10 @@
         ),
         name="attention_router",
     )(
-        starts, log_decay[0], norm_gain.reshape(heads, hd), router_new, router_old,
+        starts, log_decay[0].T, norm_gain.reshape(heads, hd), router_new.T, router_old.T,
         queries[0], keys[0], values[0],
     )
-    return logits[None], div[0, 0]
+    return logits.T[None], div[0, 0]
 
 
 def solution(mesh):

time: 103 us -> 92.7 us (0.900)
  Pallas kernels: 94.7 us -> 85.7 us
  local copies, waits for them, and re-layouts: 6.19 us -> 4.86 us
    pallas_call x1, Pallas kernels: 94.7 us -> 85.7 us  [local(): pl.pallas_call(functools.partial(body, n_dp, n_chips, n_z, tok * n_ctx *...]
    unnamed x8 -> x11, local copies, waits for them, and re-layouts: 6.19 us -> 4.86 us
where the time goes in v2:
time: 92.7 us; the launch traced here: 92.3 us
  Pallas kernels  85.7 us (92%)
  local copies, waits for them, and re-layouts  4.86 us (5%)
  between operations  1.82 us (2%)
    pallas_call x1, Pallas kernels, local(): pl.pallas_call(functools.partial(body, n_dp, n_chips, n_z, tok * n_ctx *...  85.7 us
    unnamed x11, local copies, waits for them, and re-layouts  4.86 us

profile of v2, /device:TPU:1, one launch (start us, length us, event | category | flops | bytes accessed | tf_op | source)
XLA Modules:
  0.0 92.3 jit_solution(5999959979704196663)
XLA Ops:
  0.6 0.0 copy-start
  0.6 1.0 %copy-done = bf16[8192,32]{0,1:T(8,128)(2,1)S(1)} copy-done((bf16[8192,32]{0,1:T(8,128)(2,1)S(1)}, bf16[8192,32]{0,1:T(8,128)(2,1)}, u32[]{:S(2)}) %copy-start) | copy-done | bytes 524312
  1.7 0.0 copy-start.1
  1.7 1.0 %copy-done.1 = bf16[8192,32]{0,1:T(8,128)(2,1)S(1)} copy-done((bf16[8192,32]{0,1:T(8,128)(2,1)S(1)}, bf16[8192,32]{0,1:T(8,128)(2,1)}, u32[]{:S(2)}) %copy-start.1) | copy-done | bytes 524312
  2.7 0.0 copy-start.2
  2.7 0.8 copy-done.2
  3.5 0.0 copy-start.3
  3.5 0.8 copy-done.3
  4.2 0.0 copy-start.4
  4.2 0.7 copy-done.4
  4.9 85.7 %attention_router.1 = (f32[32,192]{1,0:T(8,128)S(1)}, f32[1,128]{1,0:T(1,128)S(1)}) custom-call(s32[1,3]{1,0:T(1,128)S(1)} %copy-done.4, bf16[64,192]{1,0:T(8,128)(2,1)S(1)} %bitcast.16, f32[64,128]{1,0:T(8,128)S(1)} %bitcast.17, bf16[32,8192]{1,0:T(8,128)(2,1)S(1)} %bitcast.14, bf16[32,8192]{1,0:T(8,128)(2,1)S(1)} %bitcast.15, bf16[192,8192]{1,0:T(8,128)(2,1)} %bitcast.20, ...), custom_call_target="tpu_custom_call" | custom-call | tf_op jit(solution)/shard_map/attention_router/pallas_call | solution.py:410
  90.6 0.6 copy.12
Async XLA Ops:
  0.6 1.0 %copy-start = (bf16[8192,32]{0,1:T(8,128)(2,1)S(1)}, bf16[8192,32]{0,1:T(8,128)(2,1)}, u32[]{:S(2)}) copy-start(bf16[8192,32]{0,1:T(8,128)(2,1)} %param.14) | copy-start | bytes 1572868
  1.7 1.0 %copy-start.1 = (bf16[8192,32]{0,1:T(8,128)(2,1)S(1)}, bf16[8192,32]{0,1:T(8,128)(2,1)}, u32[]{:S(2)}) copy-start(bf16[8192,32]{0,1:T(8,128)(2,1)} %param.15) | copy-start | bytes 1572868
  2.7 0.8 copy-start.2
  3.5 0.8 copy-start.3
  4.2 0.7 copy-start.4

commit v3 on v2

--- a/solution.py
+++ b/solution.py
@@ -11,7 +11,7 @@
 F32 = jnp.float32
 BF16 = jnp.bfloat16
 NEG = -1e30
-LAG = 2
+GROUP = 2
 JOIN_LAG = 4
 Z_CHIPS = 8
 
@@ -36,7 +36,6 @@
     tok, width = q_hbm.shape
     hd = gain_ref.shape[1]
     heads = gain_ref.shape[0]
-    pair = 2 * hd
     n_y = n_chips // n_z
     dp = lax.axis_index("dp")
     me = lax.axis_index("ctx")
@@ -59,24 +58,23 @@
             device_id=(dp_to, ctx_to), device_id_type=MESH,
         )
 
+    part = width // n_y
+
+    def load_part(j):
+        cols = pl.ds(pl.multiple_of(lax.rem(my_y + j, n_y) * part, part), part)
+        return (
+            pltpu.make_async_copy(k_hbm.at[:, cols], k_buf.at[:, cols], load_sem.at[2 * j]),
+            pltpu.make_async_copy(v_hbm.at[:, cols], v_buf.at[:, cols], load_sem.at[2 * j + 1]),
+        )
+
+    for copy in load_part(0):
+        copy.start()
     small = (
         pltpu.make_async_copy(starts_hbm, starts_ref, load_sem.at[2 * n_y + 3]),
         pltpu.make_async_copy(lam_hbm, lam_ref, load_sem.at[2 * n_y + 4]),
         pltpu.make_async_copy(gain_hbm, gain_ref, load_sem.at[2 * n_y + 5]),
     )
     for copy in small:
-        copy.start()
-
-    part = width // n_y
-
-    def load_part(j):
-        cols = pl.ds(pl.multiple_of(lax.rem(my_y + j, n_y) * part, part), part)
-        return (
-            pltpu.make_async_copy(k_hbm.at[:, cols], k_buf.at[:, cols], load_sem.at[2 * j]),
-            pltpu.make_async_copy(v_hbm.at[:, cols], v_buf.at[:, cols], load_sem.at[2 * j + 1]),
-        )
-
-    for copy in load_part(0):
         copy.start()
 
     barrier = pltpu.get_barrier_semaphore()
@@ -234,17 +232,23 @@
 
     lax.fori_loop(0, n_chips, phase_two, 0)
 
-    def scan_step(src, state):
-        @pl.when(src != chip)
-        def _():
-            to = 2 * src + core
-            remote(fwd_send.at[src], fwd_recv.at[src], fwd_ssem.at[src], fwd_rsem.at[src], dp, to).wait_recv()
-            remote(a_chip.at[to], a_all.at[src], ach_ssem.at[src], ach_rsem.at[src], dp, to).wait_recv()
-
-        ret_send[src] = state.astype(BF16)
-        return a_all[src] * state + fwd_recv[src].astype(F32)
-
-    lax.fori_loop(0, n_chips, scan_step, jnp.zeros((hd, hd), F32))
+    def wait_states(i, carry):
+        src = chip_at(i, -1)
+        to = 2 * src + core
+        remote(fwd_send.at[src], fwd_recv.at[src], fwd_ssem.at[src], fwd_rsem.at[src], dp, to).wait_recv()
+        remote(a_chip.at[to], a_all.at[src], ach_ssem.at[src], ach_rsem.at[src], dp, to).wait_recv()
+        return carry
+
+    lax.fori_loop(1, n_chips, wait_states, 0)
+
+    def scan_four(i, state):
+        for j in range(4):
+            src = 4 * i + j
+            ret_send[src] = state.astype(BF16)
+            state = a_all[src] * state + fwd_recv[src].astype(F32)
+        return state
+
+    lax.fori_loop(0, n_chips // 4, scan_four, jnp.zeros((hd, hd), F32))
 
     def ret_copy(slot):
         return remote(
@@ -275,52 +279,58 @@
         meansq = jnp.mean(total * total, axis=1, keepdims=True) + 1e-06
         return split_two(total * lax.rsqrt(meansq) * gain_ref[pl.ds(h, 1), :])
 
+    def hand_over(i):
+        slot = chip_at(i, -1)
+        h = 2 * slot + core
+
+        @pl.when(i > 0)
+        def _():
+            remote(
+                ret_send.at[slot], ret_recv.at[slot], ret_ssem.at[slot], ret_rsem.at[slot], dp, 2 * slot + core
+            ).wait_recv()
+
+        first = ret_recv[slot].astype(F32)
+
+        @pl.when(core == 0)
+        def _():
+            p_buf[slot, core] = first
+            p_send[slot] = a_own[pl.ds(h, 1), :] * first + s_own[slot]
+
+        @pl.when(core == 1)
+        def _():
+            p_send[slot] = first
+            p_buf[slot, core] = a_sib[pl.ds(h, 1), :] * first + s_recv[slot].astype(F32)
+
+        p_copy(slot).start()
+
     def phase_three(i, carry):
-        @pl.when(i < n_chips)
-        def _():
-            slot = chip_at(i, -1)
-            h = 2 * slot + core
-
-            @pl.when(i > 0)
-            def _():
+        @pl.when(i < n_chips // GROUP)
+        def _():
+            for j in range(GROUP):
+                hand_over(i * GROUP + j)
+
+        @pl.when(i > 0)
+        def _():
+            slots = [chip_at((i - 1) * GROUP + j, -1) for j in range(GROUP)]
+            for slot in slots:
                 remote(
-                    ret_send.at[slot], ret_recv.at[slot], ret_ssem.at[slot], ret_rsem.at[slot], dp, 2 * slot + core
+                    p_send.at[slot], p_buf.at[slot, 1 - core], p_ssem.at[slot], p_rsem.at[slot], dp, sib
                 ).wait_recv()
-
-            first = ret_recv[slot].astype(F32)
-
-            @pl.when(core == 0)
-            def _():
-                p_buf[slot, core] = first
-                p_send[slot] = a_own[pl.ds(h, 1), :] * first + s_own[slot]
-
-            @pl.when(core == 1)
-            def _():
-                p_send[slot] = first
-                p_buf[slot, core] = a_sib[pl.ds(h, 1), :] * first + s_recv[slot].astype(F32)
-
-            p_copy(slot).start()
-
-        @pl.when(i >= LAG)
-        def _():
-            slot = chip_at(i - LAG, -1)
-            remote(
-                p_send.at[slot], p_buf.at[slot, 1 - core], p_ssem.at[slot], p_rsem.at[slot], dp, sib
-            ).wait_recv()
-            hi0, lo0 = head_out(slot, 0)
-            hi1, lo1 = head_out(slot, 1)
-            cols = pl.ds(pl.multiple_of(slot * pair, pair), pair)
-            weights = jnp.concatenate([rn_buf[:, cols], ro_buf[:, cols]], axis=0)
-            hi = jnp.concatenate([hi0, hi1], axis=1)
-            lo = jnp.concatenate([lo0, lo1], axis=1)
-            for x in (hi, lo):
-                acc_buf[...] += lax.dot_general(
-                    x, weights, (((1,), (1,)), ((), ())), preferred_element_type=F32
-                )
-
-        return carry
-
-    lax.fori_loop(0, n_chips + LAG, phase_three, 0)
+            outs = [[head_out(slot, half) for half in range(2)] for slot in slots]
+            acc = acc_buf[...]
+            for slot, (first, second) in zip(slots, outs):
+                cols = pl.ds(pl.multiple_of(slot * 2 * hd, 2 * hd), 2 * hd)
+                weights = jnp.concatenate([rn_buf[:, cols], ro_buf[:, cols]], axis=0)
+                for x, y in zip(first, second):
+                    acc = acc + lax.dot_general(
+                        jnp.concatenate([x, y], axis=1), weights, (((1,), (1,)), ((), ())),
+                        preferred_element_type=F32,
+                    )
+            acc_buf[...] = acc
+
+        return carry
+
+    lax.fori_loop(0, n_chips // GROUP + 1, phase_three, 0)
 
     n_exp = logits_ref.shape[0]
     both_logits = acc_buf[...].T
@@ -333,46 +343,17 @@
     mine = jnp.broadcast_to(jnp.sum(term, axis=1, keepdims=True), (1, 128))
     red_mine[...] = mine
 
-    def plane_copy(slot):
+    def plane_copy(dy, dz):
+        i = dy * n_z + dz
         return remote(
-            red_mine, red_plane.at[chip], plane_ssem.at[slot], plane_rsem.at[chip], dp, 2 * slot + core
+            red_mine, red_plane.at[chip], plane_ssem.at[i], plane_rsem.at[i], dp,
+            2 * (rows_of[dy] + places[dz]) + core,
         )
 
-    def send_plane(i, carry):
-        plane_copy(chip_at(i, 1)).start()
-        return carry
-
-    lax.fori_loop(1, n_chips, send_plane, 0)
+    plane_copies = [plane_copy(dy, dz) for dy in range(n_y) for dz in range(n_z) if dy or dz]
+    for copy in plane_copies:
+        copy.start()
     red_plane[chip] = mine
-
-    def add_plane(src, total):
-        @pl.when(src != chip)
-        def _():
-            remote(
-                red_mine, red_plane.at[src], plane_ssem.at[src], plane_rsem.at[src], dp, 2 * src + core
-            ).wait_recv()
-
-        return total + red_plane[src]
-
-    plane = lax.fori_loop(0, n_chips, add_plane, jnp.zeros((1, 128), F32))
-    red_part[...] = plane
-
-    def all_copy(i):
-        return remote(red_part, red_all.at[me8], all_ssem.at[i], all_rsem.at[me8], *all_peer(i))
-
-    for i in range(1, n_all):
-        all_copy(i).start()
-    red_all[me8] = plane
-    total = jnp.zeros((1, 128), F32)
-    for src in range(n_all):
-        @pl.when(src != me8)
-        def _():
-            remote(
-                red_part, red_all.at[src], all_ssem.at[src], all_rsem.at[src], src // 2, 2 * chip + src % 2
-            ).wait_recv()
-
-        total = total + red_all[src]
-    div_ref[...] = total / n_tokens
 
     def sent(i, carry):
         slot = chip_at(i, 1)
@@ -384,13 +365,27 @@
             fwd_copy(slot).wait_send()
             ret_copy(slot).wait_send()
             ach_copy(slot).wait_send()
-            plane_copy(slot).wait_send()
 
         return carry
 
     lax.fori_loop(0, n_chips, sent, 0)
-    for i in range(1, n_all):
-        all_copy(i).wait_send()
+    for copy in plane_copies:
+        copy.wait_recv()
+    plane = jnp.sum(red_plane[...], axis=0)
+    red_part[...] = plane
+
+    def all_copy(i):
+        return remote(red_part, red_all.at[me8], all_ssem.at[i], all_rsem.at[i], *all_peer(i))
+
+    all_copies = [all_copy(i) for i in range(1, n_all)]
+    for copy in all_copies:
+        copy.start()
+    red_all[me8] = plane
+    for copy in plane_copies:
+        copy.wait_send()
+    for copy in all_copies:
+        copy.wait()
+    div_ref[...] = jnp.sum(red_all[...], axis=0) / n_tokens
 
 
 def local(queries, keys, values, log_decay, starts, norm_gain, router_new, router_old):
@@ -438,7 +433,7 @@
             dma((n_chips,)), dma((n_chips,)), dma((2 * n_dp,)), dma((2 * n_dp,)),
         ],
         compiler_params=pltpu.CompilerParams(
-            collective_id=0, has_side_effects=True, vmem_limit_bytes=50 * 1024 * 1024
+            collective_id=0, has_side_effects=True, vmem_limit_bytes=63_400_000
         ),
         name="attention_router",
     )(

time: 92.7 us -> 88.9 us (0.959)
  local copies, waits for them, and re-layouts: 4.86 us -> 1.38 us
    unnamed x11 -> x1, local copies, waits for them, and re-layouts: 4.86 us -> 1.38 us
where the time goes in v3:
time: 88.9 us; the launch traced here: 88.8 us
  Pallas kernels  85 us (96%)
  between operations  2.4 us (3%)
  local copies, waits for them, and re-layouts  1.38 us (2%)
    pallas_call x1, Pallas kernels, local(): pl.pallas_call(functools.partial(body, n_dp, n_chips, n_z, tok * n_ctx *...  85 us

profile of v3, /device:TPU:1, one launch (start us, length us, event | category | flops | bytes accessed | tf_op | source)
XLA Modules:
  0.0 88.8 jit_solution(4007059848529706813)
XLA Ops:
  0.6 85.0 %attention_router.1 = (f32[32,192]{1,0:T(8,128)}, f32[1,128]{1,0:T(1,128)}) custom-call(s32[1,3]{1,0:T(1,128)} %starts_hbm.1, bf16[64,192]{1,0:T(8,128)(2,1)} %bitcast.19, f32[64,128]{1,0:T(8,128)} %bitcast.20, bf16[32,8192]{1,0:T(8,128)(2,1)} %bitcast.17, bf16[32,8192]{1,0:T(8,128)(2,1)} %bitcast.18, bf16[192,8192]{1,0:T(8,128)(2,1)} %bitcast.14, ...), custom_call_target="tpu_custom_call" | custom-call | tf_op jit(solution)/shard_map/attention_router/pallas_call | solution.py:405
  85.6 1.4 %copy.12 = f32[1,192,32]{1,2,0:T(8,128)} copy(f32[1,192,32]{1,2,0:T(8,128)} %bitcast.21) | data formatting | bytes 49152

commit v4 on v3

--- a/solution.py
+++ b/solution.py
@@ -256,7 +256,7 @@
         )
 
     def send_back(i, carry):
-        ret_copy(chip_at(i, 1)).start()
+        ret_copy(chip_at(n_chips - i, 1)).start()
         return carry
 
     lax.fori_loop(1, n_chips, send_back, 0)
@@ -280,7 +280,7 @@
         return split_two(total * lax.rsqrt(meansq) * gain_ref[pl.ds(h, 1), :])
 
     def hand_over(i):
-        slot = chip_at(i, -1)
+        slot = chip_at(lax.rem(n_chips - i, n_chips), -1)
         h = 2 * slot + core
 
         @pl.when(i > 0)
@@ -311,7 +311,7 @@
 
         @pl.when(i > 0)
         def _():
-            slots = [chip_at((i - 1) * GROUP + j, -1) for j in range(GROUP)]
+            slots = [chip_at(lax.rem(n_chips - (i - 1) * GROUP - j, n_chips), -1) for j in range(GROUP)]
             for slot in slots:
                 remote(
                     p_send.at[slot], p_buf.at[slot, 1 - core], p_ssem.at[slot], p_rsem.at[slot], dp, sib

time: 88.9 us -> 87.7 us (0.987)
  Pallas kernels: 85 us -> 83.7 us
    pallas_call x1, Pallas kernels: 85 us -> 83.7 us  [local(): pl.pallas_call(functools.partial(body, n_dp, n_chips, n_z, tok * n_ctx *...]
where the time goes in v4:
time: 87.7 us; the launch traced here: 87.5 us
  Pallas kernels  83.7 us (95%)
  between operations  2.4 us (3%)
  local copies, waits for them, and re-layouts  1.38 us (2%)
    pallas_call x1, Pallas kernels, local(): pl.pallas_call(functools.partial(body, n_dp, n_chips, n_z, tok * n_ctx *...  83.7 us

profile of v4, /device:TPU:1, one launch (start us, length us, event | category | flops | bytes accessed | tf_op | source)
XLA Modules:
  0.0 87.5 jit_solution(16056435845558084825)
XLA Ops:
  0.6 83.7 %attention_router.1 = (f32[32,192]{1,0:T(8,128)}, f32[1,128]{1,0:T(1,128)}) custom-call(s32[1,3]{1,0:T(1,128)} %starts_hbm.1, bf16[64,192]{1,0:T(8,128)(2,1)} %bitcast.19, f32[64,128]{1,0:T(8,128)} %bitcast.20, bf16[32,8192]{1,0:T(8,128)(2,1)} %bitcast.17, bf16[32,8192]{1,0:T(8,128)(2,1)} %bitcast.18, bf16[192,8192]{1,0:T(8,128)(2,1)} %bitcast.14, ...), custom_call_target="tpu_custom_call" | custom-call | tf_op jit(solution)/shard_map/attention_router/pallas_call | solution.py:405
  84.4 1.4 %copy.12 = f32[1,192,32]{1,2,0:T(8,128)} copy(f32[1,192,32]{1,2,0:T(8,128)} %bitcast.21) | data formatting | bytes 49152

commit v5 on v4

--- a/solution.py
+++ b/solution.py
@@ -80,11 +80,13 @@
     barrier = pltpu.get_barrier_semaphore()
     rows_of = [lax.rem(my_y + dy, n_y) * n_z for dy in range(n_y)]
     places = [lax.rem(my_z + dz, n_z) for dz in range(n_z)]
-    for dy in range(n_y):
-        for dz in range(n_z):
-            if dy or dz:
-                to = 2 * (rows_of[dy] + places[dz]) + core
-                pl.semaphore_signal(barrier, inc=1, device_id=(dp, to), device_id_type=MESH)
+    far_first = sorted(
+        [(dy, dz) for dy in range(n_y) for dz in range(n_z) if dy or dz],
+        key=lambda at: -min(at[0], n_y - at[0]) - min(at[1], n_z - at[1]),
+    )
+    for dy, dz in far_first:
+        to = 2 * (rows_of[dy] + places[dz]) + core
+        pl.semaphore_signal(barrier, inc=1, device_id=(dp, to), device_id_type=MESH)
     me8 = 2 * dp + core
     n_all = 2 * n_dp
 
@@ -350,7 +352,7 @@
             2 * (rows_of[dy] + places[dz]) + core,
         )
 
-    plane_copies = [plane_copy(dy, dz) for dy in range(n_y) for dz in range(n_z) if dy or dz]
+    plane_copies = [plane_copy(dy, dz) for dy, dz in far_first]
     for copy in plane_copies:
         copy.start()
     red_plane[chip] = mine

time: 87.7 us -> 87.2 us (level)
  no operation moved by 1% of the time
where the time goes in v5:
time: 87.2 us; the launch traced here: 87 us
  Pallas kernels  83.2 us (95%)
  between operations  2.4 us (3%)
  local copies, waits for them, and re-layouts  1.38 us (2%)
    pallas_call x1, Pallas kernels, local(): pl.pallas_call(functools.partial(body, n_dp, n_chips, n_z, tok * n_ctx *...  83.2 us

profile of v5, /device:TPU:1, one launch (start us, length us, event | category | flops | bytes accessed | tf_op | source)
XLA Modules:
  0.0 87.0 jit_solution(13315807805161804838)
XLA Ops:
  0.6 83.2 %attention_router.1 = (f32[32,192]{1,0:T(8,128)}, f32[1,128]{1,0:T(1,128)}) custom-call(s32[1,3]{1,0:T(1,128)} %starts_hbm.1, bf16[64,192]{1,0:T(8,128)(2,1)} %bitcast.19, f32[64,128]{1,0:T(8,128)} %bitcast.20, bf16[32,8192]{1,0:T(8,128)(2,1)} %bitcast.17, bf16[32,8192]{1,0:T(8,128)(2,1)} %bitcast.18, bf16[192,8192]{1,0:T(8,128)(2,1)} %bitcast.14, ...), custom_call_target="tpu_custom_call" | custom-call | tf_op jit(solution)/shard_map/attention_router/pallas_call | solution.py:407
  83.9 1.4 %copy.12 = f32[1,192,32]{1,2,0:T(8,128)} copy(f32[1,192,32]{1,2,0:T(8,128)} %bitcast.21) | data formatting | bytes 49152
